TPU v7x, 128 devices: a whole 4x4x4 slice. The times are simulated.
128 devices in a mesh: lon: 16 (over z_hi, y, core), lat: 8 (over z_lo, x).
Axes of the slice: x: 4, y: 4, z: 4 (z_hi: 2, z_lo: 2; z = z_hi * 2 + z_lo), core: 2. Of those that a mesh axis runs over, the one named last changes fastest.
Arguments:
- coarse: float32 [12, 64, 3072], P(None, 'lat', 'lon'), may hold values from -100 to 100
- static: float32 [4, 64, 3072], P(None, 'lat', 'lon'), may hold values from -16 to 16
- noise_seeds: int32 [64], replicated, may hold values from 0 to 1073741823
- regress_in: bfloat16 [3, 3, 16, 128], replicated, may hold values from -0.5 to 0.5
- regress_one: bfloat16 [3, 3, 128, 128], replicated, may hold values from -0.1875 to 0.1875
- regress_two: bfloat16 [3, 3, 128, 128], replicated, may hold values from -0.1875 to 0.1875
- regress_out: bfloat16 [3, 3, 128, 12], replicated, may hold values from -0.1875 to 0.1875
- diffuse_in: bfloat16 [3, 3, 40, 256], replicated, may hold values from -0.3125 to 0.3125
- diffuse_one: bfloat16 [3, 3, 256, 256], replicated, may hold values from -0.125 to 0.125
- diffuse_two: bfloat16 [3, 3, 256, 256], replicated, may hold values from -0.125 to 0.125
- diffuse_out: bfloat16 [3, 3, 256, 12], replicated, may hold values from -0.125 to 0.125
Outputs:
- mean_field: float32 [12, 64, 3072], P(None, 'lat', 'lon')
- field: float32 [12, 64, 3072], P(None, 'lat', 'lon')
All inputs are finite; a program needn't handle non-finite values.
Results may differ from a plain program's by a relative error of at most 0.0034.
The roundings to bfloat16 on the way count: a program that leaves them out, or rounds other values in their place, can miss the bound.
Values may be sent and summed in bfloat16 or wider, within the bound.
A program may use at most 64 MiB of HBM per device.

v0:
```python
import functools

import jax
import jax.numpy as jnp
from jax import lax
from jax.experimental import pallas as pl
from jax.experimental.pallas import tpu as pltpu
from jax.sharding import PartitionSpec as P

MESH = pl.DeviceIdType.MESH
F32 = jnp.float32
BF16 = jnp.bfloat16

LON, LAT = 16, 8
ALL = LON * LAT
ROWS = 8
COLS = 192
BAND_ROWS = ROWS * LAT
BAND_COLS = COLS * LON
MARGIN = 32
PATCH = COLS + 2 * MARGIN
SIDE = 40
W = COLS + 2 * SIDE
OFF = SIDE - MARGIN
FRAME = 3 * ROWS
CH = 16
REG = 128
DIF = 256
OUTC = 12
EPS = 1e-05

AROUND = ((0, -1), (0, 1), (-1, -1), (-1, 0), (-1, 1), (1, -1), (1, 0), (1, 1))


def hashed(value):
    for _ in range(2):
        value = value ^ (lax.shift_right_logical(value, 16))
        value = value * 73244475
    return value ^ (lax.shift_right_logical(value, 16))


def at_row(row, width):
    return pl.multiple_of(row * width, 16)


def all_groups(stats, size):
    lane = lax.broadcasted_iota(jnp.int32, stats.shape, 1)
    step = 1
    while step < size:
        up = pltpu.roll(stats, 128 - step, axis=1)
        down = pltpu.roll(stats, step, axis=1)
        stats = stats + jnp.where((lane // step) % 2 == 0, up, down)
        step *= 2
    return stats


def scale_shift(sums, squares, count):
    mean = sums / count
    scale = lax.rsqrt(squares / count - mean * mean + EPS)
    return 0.5 * scale, -0.5 * scale * mean


def half_silu(half):
    return half + half * jnp.tanh(half)


def fold(values):
    return jnp.sum(values.reshape(values.shape[0] // 8, 8, values.shape[1]), axis=0)


def kernel(
    coarse,
    static,
    seeds,
    w_in,
    w_one_hbm,
    w_two_hbm,
    w_out,
    d_in,
    d_one_hbm,
    d_two_hbm,
    d_out,
    mean_out,
    field_out,
    w_one,
    w_two,
    d_one,
    d_two,
    own32,
    own16,
    tall,
    wide,
    xw,
    wb_in,
    wb_patch,
    wb_mean,
    wb_vel,
    first,
    second,
    third,
    act,
    noise_keep,
    parts,
    partial,
    mean_acc,
    p_first,
    p_second,
    p_third,
    p_act,
    pad32,
    edge_send,
    edge_recv,
    stat_send,
    stat_one,
    stat_two,
    stat_three,
    stat_four,
    w_sem,
    in_send,
    in_recv,
    st_send,
    st_recv,
    e_send,
    e_recv,
):
    lon = lax.axis_index("lon")
    lat = lax.axis_index("lat")
    me = lon * LAT + lat

    def partner(step):
        other = lax.rem(me + step, ALL)
        return {"lon": other // LAT, "lat": lax.rem(other, LAT)}

    def row_ok(e):
        row = lat * ROWS - ROWS + e
        return jnp.where((row >= 0) & (row < BAND_ROWS), 1.0, 0.0).astype(F32)

    loads = [
        pltpu.make_async_copy(src, dst, w_sem.at[i])
        for i, (src, dst) in enumerate(
            ((w_one_hbm, w_one), (w_two_hbm, w_two), (d_one_hbm, d_one), (d_two_hbm, d_two))
        )
    ]
    for load in loads:
        load.start()
    barrier = pltpu.get_barrier_semaphore()

    def greet(step, carry):
        pl.semaphore_signal(barrier, inc=1, device_id=partner(step), device_id_type=MESH)
        return carry

    lax.fori_loop(1, ALL, greet, 0)

    own32[...] = jnp.zeros_like(own32)
    for r in range(ROWS):
        own32[r * CH : r * CH + 12, 0:COLS] = coarse[:, r, :]
        own32[r * CH + 12 : r * CH + 16, 0:COLS] = static[:, r, :]
    own16[...] = own32[...].astype(BF16)

    wb_in[...] = jnp.zeros_like(wb_in)
    for p in range(6):
        for dy in range(3):
            for dx in range(3):
                at = dx * 128 + (p + dy) * CH
                wb_in[at : at + CH, p * REG : (p + 1) * REG] = w_in[dy * 3 + dx]
    wb_patch[...] = jnp.zeros_like(wb_patch)
    low_rows = lax.broadcasted_iota(jnp.int32, (40, DIF), 0) < OUTC
    for dy in range(3):
        for dx in range(3):
            raw = d_in[dy * 3 + dx].astype(F32)
            pieces = (
                jnp.where(low_rows, raw, 0.0)[:CH].astype(BF16),
                raw[24:40].astype(BF16),
                jnp.where(low_rows, pltpu.roll(raw, 28, axis=0), 0.0)[:CH].astype(BF16),
            )
            for part, piece in enumerate(pieces):
                for p in range(6):
                    at = part * 384 + dx * 128 + (p + dy) * CH
                    wb_patch[at : at + CH, p * DIF : (p + 1) * DIF] = piece
    pad32[...] = jnp.zeros_like(pad32)
    lane256 = lax.broadcasted_iota(jnp.int32, (1, 256), 1)
    lane128 = lax.broadcasted_iota(jnp.int32, (1, 128), 1)
    for dx in range(3):
        base = jnp.zeros((REG, 128), F32)
        for dy in range(3):
            pad32[0:REG, 0:OUTC] = w_out[dy * 3 + dx].astype(F32)
            base = base + pltpu.roll(pad32[0:REG, :], (2 - dy) * CH, axis=1)
        base = jnp.concatenate([base, jnp.zeros((REG, 128), F32)], axis=1)
        for e in range(3, 21):
            moved = pltpu.roll(base, ((e - 5) * CH) % 256, axis=1)
            if e < 5:
                moved = jnp.where(lane256 < (e - 2) * CH, moved, 0.0)
            if e > 18:
                moved = jnp.where(lane256 >= (e - 5) * CH, moved, 0.0)
            wb_mean[(e - 3) * REG : (e - 2) * REG, dx * 256 : (dx + 1) * 256] = moved.astype(BF16)
    for dx in range(3):
        base = jnp.zeros((DIF, 128), F32)
        for dy in range(3):
            pad32[:, 0:OUTC] = d_out[dy * 3 + dx].astype(F32)
            base = base + pltpu.roll(pad32[...], (2 - dy) * CH, axis=1)
        for e in range(7, 17):
            moved = pltpu.roll(base, ((e - 9) * CH) % 128, axis=1)
            if e < 9:
                moved = jnp.where(lane128 < (e - 6) * CH, moved, 0.0)
            if e > 14:
                moved = jnp.where(lane128 >= (e - 9) * CH, moved, 0.0)
            wb_vel[(e - 7) * DIF : (e - 6) * DIF, dx * 128 : (dx + 1) * 128] = moved.astype(BF16)

    lane_row = lane256 // CH
    lane_ok = jnp.zeros((1, 256), F32)
    seed = jnp.zeros((1, 256), jnp.int32)
    for r in range(16):
        row = lat * ROWS - 4 + r
        here = seeds[jnp.clip(row, 0, BAND_ROWS - 1)]
        seed = jnp.where(lane_row == r, here, seed)
        lane_ok = jnp.where(lane_row == r, row_ok(4 + r), lane_ok)

    def shift(values, dx):
        count = values.shape[0]
        spot = lax.broadcasted_iota(jnp.int32, values.shape, 0)
        if dx == 0:
            return jnp.where(spot == 0, 0.0, pltpu.roll(values, 1, axis=0))
        if dx == 2:
            return jnp.where(spot == count - 1, 0.0, pltpu.roll(values, count - 1, axis=0))
        return values

    def put_part(part, values):
        for dx in range(3):
            moved = shift(values, dx)
            at = part * 384 + dx * 128
            parts[0, :, at : at + 128] = moved[:, :128].astype(BF16)
            parts[1, :, at : at + 128] = pltpu.roll(moved, 192, axis=1)[:, :128].astype(BF16)
            parts[2, :, at : at + 128] = moved[:, 128:].astype(BF16)

    def noise_rows(i, carry):
        at = pl.multiple_of(i * 32, 32)
        column = lon * COLS - MARGIN + at + lax.broadcasted_iota(jnp.int32, (32, 256), 0)
        column = jnp.where(column < 0, column + BAND_COLS, column)
        column = jnp.where(column >= BAND_COLS, column - BAND_COLS, column)
        channel = lax.broadcasted_iota(jnp.int32, (32, 256), 1) % CH
        start = seed ^ ((column * OUTC + channel) * 1640531527)
        total = jnp.zeros((32, 256), jnp.int32)
        for turn in range(4):
            total = total + (hashed(start + turn * 374761393) & 65535)
        uniform = total.astype(F32) * (1.0 / 65536.0) + 4.0 / 131072.0
        noise_keep[pl.ds(at, 32), :] = (uniform - 2.0) * 1.7320508075688772 * lane_ok
        return carry

    lax.fori_loop(0, PATCH // 32, noise_rows, 0)
    put_part(0, noise_keep[...])

    pl.semaphore_wait(barrier, ALL - 1)

    def around(k):
        dlon, dlat = AROUND[k]
        target = {"lon": lax.rem(lon + dlon + LON, LON), "lat": lax.rem(lat + dlat + LAT, LAT)}
        if dlon == 0:
            src, dst = own16, tall.at[k]
        elif dlon == 1:
            src, dst = own16.at[:, 128:256], wide.at[k - 2]
        else:
            src, dst = own16.at[:, 0:128], wide.at[k - 2]
        return pltpu.make_async_remote_copy(
            src_ref=src,
            dst_ref=dst,
            send_sem=in_send.at[k],
            recv_sem=in_recv.at[k],
            device_id=target,
            device_id_type=MESH,
        )

    order = (2, 4, 5, 7, 3, 6, 0, 1)
    copies = {k: around(k) for k in order}
    for k in order:
        copies[k].start()
    for k in order:
        copies[k].wait_recv()

    def assemble(centre, left, right):
        lane = lax.broadcasted_iota(jnp.int32, (128, 384), 1)
        zeros = jnp.zeros((128, 128), F32)
        mid = pltpu.roll(jnp.concatenate([centre, zeros], axis=1), SIDE, axis=1)
        low = pltpu.roll(jnp.concatenate([left, zeros, zeros], axis=1), 384 - 24, axis=1)
        high = pltpu.roll(jnp.concatenate([right, zeros, zeros], axis=1), SIDE + COLS, axis=1)
        inner = jnp.where(lane < SIDE + COLS, mid, jnp.where(lane < W, high, 0.0))
        return jnp.where(lane < SIDE, low, inner)

    up = assemble(tall[1].astype(F32), wide[7 - 2].astype(F32), wide[4 - 2].astype(F32))
    mid = assemble(own16[...].astype(F32), wide[6 - 2].astype(F32), wide[3 - 2].astype(F32))
    down = assemble(tall[0].astype(F32), wide[5 - 2].astype(F32), wide[2 - 2].astype(F32))
    up = jnp.where(lat == 0, 0.0, up)
    down = jnp.where(lat == LAT - 1, 0.0, down)
    xt = jnp.concatenate([up.T, mid.T, down.T], axis=1)[:W]
    xt_far = pltpu.roll(xt, 320, axis=1)
    for dx in range(3):
        if dx == 0:
            near, far = pltpu.roll(xt, 1, axis=0), pltpu.roll(xt_far, 1, axis=0)
        elif dx == 2:
            near, far = pltpu.roll(xt, W - 1, axis=0), pltpu.roll(xt_far, W - 1, axis=0)
        else:
            near, far = xt, xt_far
        for win in range(5):
            source = (near, far)[win % 2]
            at = (win // 2) * 128
            xw[win, :, dx * 128 : (dx + 1) * 128] = source[:, at : at + 128].astype(BF16)

    def first_rows(win, low, high):
        out = jnp.dot(
            xw[win], wb_in[:, low * REG : high * REG], preferred_element_type=F32
        ).astype(BF16)
        s = jnp.zeros((8, REG), F32)
        q = jnp.zeros((8, REG), F32)
        for p in range(low, high):
            e = win * 4 + 1 + p
            row = out[:, (p - low) * REG : (p - low + 1) * REG]
            first[e * W : (e + 1) * W, :] = row
            if 8 <= e < 16:
                cell = row[SIDE : SIDE + COLS].astype(F32)
                s = s + fold(cell)
                q = q + fold(cell * cell)
        return s, q

    def send_band(which, s, q, recv):
        stat_send[which, 0:1, :] = jnp.sum(s, axis=0, keepdims=True)
        stat_send[which, 1:2, :] = jnp.sum(q, axis=0, keepdims=True)

        def one(step, carry):
            pltpu.make_async_remote_copy(
                src_ref=stat_send.at[which, pl.ds(0, 2)],
                dst_ref=recv.at[step - 1],
                send_sem=st_send.at[which],
                recv_sem=st_recv.at[which],
                device_id=partner(step),
                device_id_type=MESH,
            ).start()
            return carry

        lax.fori_loop(1, ALL, one, 0)

    def band_scale(which, recv):
        pltpu.make_async_copy(recv, recv, st_recv.at[which]).wait()
        stat_send[4 + which, 0:2, :] = stat_send[which, 0:2, :] + jnp.sum(recv[...], axis=0)
        total = all_groups(stat_send[4 + which], REG // 32)
        return scale_shift(
            total[0:1], total[1:2], float(BAND_ROWS * BAND_COLS * (REG // 32))
        )

    def send_patch(which, s, q, recv):
        s = jnp.sum(s, axis=0, keepdims=True)
        q = jnp.sum(q, axis=0, keepdims=True)
        stat_send[which, 0:1, :] = s[:, :128]
        stat_send[which, 1:2, :] = s[:, 128:]
        stat_send[which, 2:3, :] = q[:, :128]
        stat_send[which, 3:4, :] = q[:, 128:]
        for step in range(1, LAT):
            pltpu.make_async_remote_copy(
                src_ref=stat_send.at[which, pl.ds(0, 4)],
                dst_ref=recv.at[step - 1],
                send_sem=st_send.at[which],
                recv_sem=st_recv.at[which],
                device_id={"lat": lax.rem(lat + step, LAT)},
                device_id_type=MESH,
            ).start()

    def patch_scale(which, recv):
        pltpu.make_async_copy(recv, recv, st_recv.at[which]).wait()
        stat_send[4 + which, 0:4, :] = stat_send[which, 0:4, :] + jnp.sum(recv[...], axis=0)
        total = all_groups(stat_send[4 + which], DIF // 32)
        sums = jnp.concatenate([total[0:1], total[1:2]], axis=1)
        squares = jnp.concatenate([total[2:3], total[3:4]], axis=1)
        return scale_shift(sums, squares, float(BAND_ROWS * PATCH * (DIF // 32)))

    stats = [first_rows(1, 3, 6), first_rows(2, 2, 4), first_rows(3, 0, 3)]
    stat_send[...] = jnp.zeros_like(stat_send)
    send_band(0, sum(s for s, _ in stats), sum(q for _, q in stats), stat_one)

    first_rows(0, 0, 6)
    first_rows(1, 2, 3)
    first_rows(3, 3, 6)
    first_rows(4, 2, 6)
    own_xt = xt_far[OFF : OFF + PATCH, :256]
    put_part(1, own_xt)

    def patch_rows(win):
        return ((3, 6), (2, 4), (0, 3))[win]

    def rest_rows(win):
        return ((0, 3), None, (3, 6))[win]

    for win in range(3):
        for span in (patch_rows(win), rest_rows(win)):
            if span is None:
                continue
            low, high = span
            out = jnp.dot(
                parts[win, :, 0:768],
                wb_patch[0:768, low * DIF : high * DIF],
                preferred_element_type=F32,
            )
            for p in range(low, high):
                e = win * 4 + 5 + p
                partial[(e - 5) * PATCH : (e - 4) * PATCH, :] = out[
                    :, (p - low) * DIF : (p - low + 1) * DIF
                ]

    def activate_band(source, a, b, e):
        ok = row_ok(e)
        at = at_row(e, W)
        half = source[pl.ds(at, W), :].astype(F32) * (a * ok) + b * ok
        out = half_silu(half)
        act[0, pl.ds(at, W), :] = pltpu.roll(out, 1, axis=0).astype(BF16)
        act[1, pl.ds(at, W), :] = out.astype(BF16)
        act[2, pl.ds(at, W), :] = pltpu.roll(out, W - 1, axis=0).astype(BF16)

    def loop(count, body):
        lax.fori_loop(0, count, lambda i, c: (body(i), c)[1], 0)

    def conv_band(weight, e, rows):
        lhs = jnp.concatenate(
            [
                act[dx, pl.ds(at_row(e + dy - 1, W), rows * W), :]
                for dy in range(3)
                for dx in range(3)
            ],
            axis=1,
        )
        return jnp.dot(lhs, weight[...], preferred_element_type=F32)

    a, b = band_scale(0, stat_one)
    loop(10, lambda i: activate_band(first, a, b, i + 7))
    loads[0].wait()

    def second_own(i, carry):
        s, q = carry
        e = 8 + i
        out = conv_band(w_one, e, 1).astype(BF16)
        second[pl.ds(at_row(e, W), W), :] = out
        cell = out[SIDE : SIDE + COLS].astype(F32)
        return s + fold(cell), q + fold(cell * cell)

    zero = jnp.zeros((8, REG), F32)
    s, q = lax.fori_loop(0, ROWS, second_own, (zero, zero))
    send_band(1, s, q, stat_two)

    def second_rest(i):
        e = 2 + i + (i // 6) * 8
        second[pl.ds(at_row(e, W), W), :] = conv_band(w_one, e, 1).astype(BF16)

    loop(12, lambda i: activate_band(first, a, b, 1 + i + (i // 6) * 10))
    loop(12, second_rest)

    a2, b2 = band_scale(1, stat_two)
    loop(14, lambda i: activate_band(second, a2, b2, i + 5))
    loads[1].wait()

    def third_row(e):
        at = at_row(e, W)
        out = first[pl.ds(at, W), :].astype(F32) + conv_band(w_two, e, 1)
        third[pl.ds(at, W), :] = (out * row_ok(e)).astype(BF16)

    loop(12, lambda i: third_row(i + 6))

    def mean_terms(low, high):
        lhs = jnp.concatenate([third[e * W : (e + 1) * W, :] for e in range(low, high)], axis=1)
        return [
            jnp.dot(
                lhs,
                wb_mean[(low - 3) * REG : (high - 3) * REG, dx * 256 : (dx + 1) * 256],
                preferred_element_type=F32,
            )
            for dx in range(3)
        ]

    def put_mean():
        total = (
            pltpu.roll(mean_acc[0], 1, axis=0)
            + mean_acc[1]
            + pltpu.roll(mean_acc[2], W - 1, axis=0)
        )[OFF : OFF + PATCH]
        put_part(2, total * lane_ok)
        return total

    def patch_first_rows(win, span):
        low, high = span
        out = jnp.dot(
            parts[win, :, 768:1152],
            wb_patch[768:1152, low * DIF : high * DIF],
            preferred_element_type=F32,
        )
        s = jnp.zeros((8, DIF), F32)
        q = jnp.zeros((8, DIF), F32)
        for p in range(low, high):
            e = win * 4 + 5 + p
            at = (e - 5) * PATCH
            row = out[:, (p - low) * DIF : (p - low + 1) * DIF] + partial[at : at + PATCH, :]
            row = row.astype(BF16)
            p_first[at : at + PATCH, :] = row
            if 8 <= e < 16:
                cell = row.astype(F32)
                s = s + fold(cell)
                q = q + fold(cell * cell)
        return s, q

    for dx, term in enumerate(mean_terms(6, 18)):
        mean_acc[dx] = term
    put_mean()
    stats = [patch_first_rows(win, patch_rows(win)) for win in range(3)]
    send_patch(2, sum(s for s, _ in stats), sum(q for _, q in stats), stat_three)

    def activate_rest(i):
        activate_band(second, a2, b2, 2 + i + (i // 3) * 14)

    loop(6, activate_rest)
    loop(6, lambda i: third_row(3 + i + (i // 3) * 12))
    for low, high in ((3, 6), (18, 21)):
        for dx, term in enumerate(mean_terms(low, high)):
            mean_acc[dx] = mean_acc[dx] + term
    mean_all = put_mean()
    mean_own = pltpu.roll(mean_all, 192, axis=1)[:, :128]
    noise_own = pltpu.roll(noise_keep[...], 192, axis=1)[:, :128]
    base = mean_own + noise_own

    def put_out(out_ref, values):
        flat = pltpu.roll(values.T, PATCH - MARGIN, axis=1)[:, :COLS]
        for r in range(ROWS):
            out_ref[:, r, :] = flat[r * CH : r * CH + OUTC, :]

    put_out(mean_out, mean_own)
    pad32[...] = base
    patch_first_rows(0, rest_rows(0))
    patch_first_rows(2, rest_rows(2))

    def activate_patch(source, shift_row, a, b, e):
        ok = row_ok(e)
        half = source[pl.ds(at_row(e - shift_row, PATCH), PATCH), :].astype(F32) * (a * ok) + b * ok
        out = half_silu(half)
        at = at_row(e - 5, PATCH)
        for dx in range(3):
            p_act[dx, pl.ds(at, PATCH), :] = shift(out, dx).astype(BF16)

    def conv_patch(weight, e):
        lhs = jnp.concatenate(
            [
                p_act[dx, pl.ds(at_row(e + dy - 6, PATCH), PATCH), :]
                for dy in range(3)
                for dx in range(3)
            ],
            axis=1,
        )
        return jnp.dot(lhs, weight[...], preferred_element_type=F32)

    a3, b3 = patch_scale(2, stat_three)
    loop(10, lambda i: activate_patch(p_first, 5, a3, b3, i + 7))
    loads[2].wait()

    def p_second_own(i, carry):
        s, q = carry
        e = 8 + i
        out = conv_patch(d_one, e).astype(BF16)
        p_second[pl.ds(at_row(e - 6, PATCH), PATCH), :] = out
        cell = out.astype(F32)
        return s + fold(cell), q + fold(cell * cell)

    zero = jnp.zeros((8, DIF), F32)
    s, q = lax.fori_loop(0, ROWS, p_second_own, (zero, zero))
    send_patch(3, s, q, stat_four)

    def p_second_rest(i):
        e = 6 + i + (i // 2) * 8
        p_second[pl.ds(at_row(e - 6, PATCH), PATCH), :] = conv_patch(d_one, e).astype(BF16)

    loop(4, lambda i: activate_patch(p_first, 5, a3, b3, 5 + i + (i // 2) * 10))
    loop(4, p_second_rest)

    a4, b4 = patch_scale(3, stat_four)
    loop(12, lambda i: activate_patch(p_second, 6, a4, b4, i + 6))
    loads[3].wait()

    def p_third_row(i):
        e = 7 + i
        out = p_first[pl.ds(at_row(e - 5, PATCH), PATCH), :].astype(F32) + conv_patch(d_two, e)
        p_third[pl.ds(at_row(e - 7, PATCH), PATCH), :] = (out * row_ok(e)).astype(BF16)

    loop(10, p_third_row)

    lhs = jnp.concatenate([p_third[e * PATCH : (e + 1) * PATCH, :] for e in range(10)], axis=1)
    out = jnp.dot(lhs, wb_vel[...], preferred_element_type=F32)
    velocity = shift(out[:, 0:128], 0) + out[:, 128:256] + shift(out[:, 256:384], 2)
    edge_send[0] = velocity[0:MARGIN]
    edge_send[1] = velocity[PATCH - MARGIN : PATCH]
    edges = [
        pltpu.make_async_remote_copy(
            src_ref=edge_send.at[k],
            dst_ref=edge_recv.at[k],
            send_sem=e_send.at[k],
            recv_sem=e_recv.at[k],
            device_id={"lon": lax.rem(lon + LON + step, LON)},
            device_id_type=MESH,
        )
        for k, step in ((0, -1), (1, 1))
    ]
    for edge in edges:
        edge.start()
    for k in order:
        copies[k].wait_send()
    for which, recv in enumerate((stat_one, stat_two, stat_three, stat_four)):
        pltpu.make_async_copy(recv, recv, st_send.at[which]).wait()
    for edge in edges:
        edge.wait()
    from_left = velocity[MARGIN : 2 * MARGIN] + edge_recv[1]
    from_right = velocity[COLS : COLS + MARGIN] + edge_recv[0]
    total = jnp.concatenate(
        [
            velocity[0:MARGIN],
            from_left * 0.5,
            velocity[2 * MARGIN : COLS],
            from_right * 0.5,
            velocity[COLS + MARGIN :],
        ],
        axis=0,
    )
    put_out(field_out, pad32[...] + total)


def on_device(coarse, static, noise_seeds, w_in, w_one, w_two, w_out, d_in, d_one, d_two, d_out):
    vmem = pl.BlockSpec(memory_space=pltpu.VMEM)
    smem = pl.BlockSpec(memory_space=pltpu.SMEM)
    hbm = pl.BlockSpec(memory_space=pl.ANY)
    out = jax.ShapeDtypeStruct((OUTC, ROWS, COLS), F32)
    return pl.pallas_call(
        kernel,
        out_shape=(out, out),
        in_specs=[vmem, vmem, smem, vmem, hbm, hbm, vmem, vmem, hbm, hbm, vmem],
        out_specs=(vmem, vmem),
        scratch_shapes=[
            pltpu.VMEM((9 * REG, REG), BF16),
            pltpu.VMEM((9 * REG, REG), BF16),
            pltpu.VMEM((9 * DIF, DIF), BF16),
            pltpu.VMEM((9 * DIF, DIF), BF16),
            pltpu.VMEM((128, 256), F32),
            pltpu.VMEM((128, 256), BF16),
            pltpu.VMEM((2, 128, 256), BF16),
            pltpu.VMEM((6, 128, 128), BF16),
            pltpu.VMEM((5, W, 384), BF16),
            pltpu.VMEM((384, 6 * REG), BF16),
            pltpu.VMEM((1152, 6 * DIF), BF16),
            pltpu.VMEM((18 * REG, 768), BF16),
            pltpu.VMEM((10 * DIF, 384), BF16),
            pltpu.VMEM((FRAME * W, REG), BF16),
            pltpu.VMEM((FRAME * W, REG), BF16),
            pltpu.VMEM((FRAME * W, REG), BF16),
            pltpu.VMEM((3, FRAME * W, REG), BF16),
            pltpu.VMEM((PATCH, 256), F32),
            pltpu.VMEM((3, PATCH, 1152), BF16),
            pltpu.VMEM((14 * PATCH, DIF), F32),
            pltpu.VMEM((3, W, 256), F32),
            pltpu.VMEM((14 * PATCH, DIF), BF16),
            pltpu.VMEM((12 * PATCH, DIF), BF16),
            pltpu.VMEM((10 * PATCH, DIF), BF16),
            pltpu.VMEM((3, 14 * PATCH, DIF), BF16),
            pltpu.VMEM((256, 128), F32),
            pltpu.VMEM((2, MARGIN, 128), F32),
            pltpu.VMEM((2, MARGIN, 128), F32),
            pltpu.VMEM((8, 8, 128), F32),
            pltpu.VMEM((ALL - 1, 2, 128), F32),
            pltpu.VMEM((ALL - 1, 2, 128), F32),
            pltpu.VMEM((LAT - 1, 4, 128), F32),
            pltpu.VMEM((LAT - 1, 4, 128), F32),
            pltpu.SemaphoreType.DMA((4,)),
            pltpu.SemaphoreType.DMA((8,)),
            pltpu.SemaphoreType.DMA((8,)),
            pltpu.SemaphoreType.DMA((4,)),
            pltpu.SemaphoreType.DMA((4,)),
            pltpu.SemaphoreType.DMA((2,)),
            pltpu.SemaphoreType.DMA((2,)),
        ],
        compiler_params=pltpu.CompilerParams(
            collective_id=0, has_side_effects=True, vmem_limit_bytes=60 * 1024 * 1024
        ),
    )(
        coarse,
        static,
        noise_seeds,
        w_in.reshape(9, CH, REG),
        w_one.reshape(9 * REG, REG),
        w_two.reshape(9 * REG, REG),
        w_out.reshape(9, REG, OUTC),
        d_in.reshape(9, 40, DIF),
        d_one.reshape(9 * DIF, DIF),
        d_two.reshape(9 * DIF, DIF),
        d_out.reshape(9, DIF, OUTC),
    )


def solution(mesh):
    brick = P(None, "lat", "lon")
    return jax.shard_map(
        on_device,
        mesh=mesh,
        in_specs=(brick, brick) + (P(),) * 9,
        out_specs=(brick, brick),
        check_vma=False,
    )
```

profile of v0, /device:TPU:1, one launch (start us, length us, event | category | flops | bytes accessed | tf_op | source)
XLA Modules:
  0.0 77.5 jit_solution(1599364002001133868)
XLA Ops:
  0.6 1.7 %copy.13 = bf16[3,3,128,12]{3,2,1,0:T(8,128)(2,1)} copy(bf16[3,3,128,12]{2,3,1,0:T(8,128)(2,1)} %param.17) | data formatting | bytes 55296 | tf_op args[6]
  2.3 2.0 %copy.14 = bf16[3,3,256,12]{3,2,1,0:T(8,128)(2,1)} copy(bf16[3,3,256,12]{2,3,1,0:T(8,128)(2,1)} %param.21) | data formatting | bytes 110592 | tf_op args[10]
  4.3 70.1 %shard_map.122 = (f32[12,8,192]{2,1,0:T(8,128)}, f32[12,8,192]{2,1,0:T(8,128)}) custom-call(f32[12,8,192]{2,1,0:T(8,128)} %coarse.1, f32[4,8,192]{2,1,0:T(8,128)} %static.1, s32[64]{0:T(128)} %seeds.1, bf16[9,16,128]{2,1,0:T(8,128)(2,1)} %bitcast.15, bf16[1152,128]{1,0:T(8,128)(2,1)} %bitcast.12, bf16[1152,128]{1,0:T(8,128)(2,1)} %bitcast.13, ...), custom_call_target="tpu_custom_call" | custom-call | tf_op jit(solution)/shard_map/pallas_call | solution.py:630
  74.4 1.5 %copy.17 = f32[12,8,192]{2,1,0:T(8,128)} copy(f32[12,8,192]{2,1,0:T(8,128)} %get-tuple-element.4) | data formatting | bytes 147456
  76.0 1.5 %copy.18 = f32[12,8,192]{2,1,0:T(8,128)} copy(f32[12,8,192]{2,1,0:T(8,128)} %get-tuple-element.5) | data formatting | bytes 147456
where the time goes:
time: 78.3 us; the launch traced here: 77.5 us
  Pallas kernels  70.1 us (90%)
  local copies, waits for them, and re-layouts  6.75 us (9%)
    pallas_call x1, Pallas kernels, on_device(): pl.pallas_call(kernel, out_shape=(out, out), in_specs=[vmem, vmem, smem,...  70.1 us
    unnamed x4, local copies, waits for them, and re-layouts  6.75 us

commit v1 on v0

--- a/solution.py
+++ b/solution.py
@@ -27,6 +27,7 @@
 REG = 128
 DIF = 256
 OUTC = 12
+STEPS = (2, 1, 3, 0)
 EPS = 1e-05
 
 AROUND = ((0, -1), (0, 1), (-1, -1), (-1, 0), (-1, 1), (1, -1), (1, 0), (1, 1))
@@ -69,8 +70,8 @@
 
 
 def kernel(
-    coarse,
-    static,
+    coarse_hbm,
+    static_hbm,
     seeds,
     w_in,
     w_one_hbm,
@@ -82,6 +83,8 @@
     d_out,
     mean_out,
     field_out,
+    coarse,
+    static,
     w_one,
     w_two,
     d_one,
@@ -108,6 +111,7 @@
     p_third,
     p_act,
     pad32,
+    taps,
     edge_send,
     edge_recv,
     stat_send,
@@ -125,32 +129,78 @@
 ):
     lon = lax.axis_index("lon")
     lat = lax.axis_index("lat")
-    me = lon * LAT + lat
-
-    def partner(step):
-        other = lax.rem(me + step, ALL)
-        return {"lon": other // LAT, "lat": lax.rem(other, LAT)}
+
+    core = lax.rem(lon, 2)
+    y = lax.rem(lon // 2, 4)
+    x = lax.rem(lat, 4)
+    z = (lon // 8) * 2 + lat // 4
+
+    def chip(dz, dy, dx):
+        there = lax.rem(z + dz, 4)
+        far_lon = (there // 2) * 8 + lax.rem(y + dy, 4) * 2
+        return far_lon, lax.rem(there, 2) * 4 + lax.rem(x + dx, 4)
+
+    def reach(i):
+        return jnp.where(i == 0, 2, jnp.where(i == 3, 0, jnp.where(i == 1, 1, 3)))
+
+    def to_all(action):
+        def some(i, carry):
+            dz, dy = reach(i // 4), reach(lax.rem(i, 4))
+            for j, dx in enumerate(STEPS):
+                far_lon, far_lat = chip(dz, dy, dx)
+                for k in range(2):
+                    target = {"lon": far_lon + (1 - core if k == 0 else core), "lat": far_lat}
+                    action(target, i * 8 + j * 2 + k)
+            return carry
+
+        lax.fori_loop(0, 15, some, 0)
+        for j, dx in enumerate(STEPS):
+            far_lon, far_lat = chip(0, 0, dx)
+            for k in range(2):
+                if (j, k) != (3, 1):
+                    target = {"lon": far_lon + (1 - core if k == 0 else core), "lat": far_lat}
+                    action(target, 120 + j * 2 + k)
 
     def row_ok(e):
         row = lat * ROWS - ROWS + e
         return jnp.where((row >= 0) & (row < BAND_ROWS), 1.0, 0.0).astype(F32)
 
-    loads = [
-        pltpu.make_async_copy(src, dst, w_sem.at[i])
-        for i, (src, dst) in enumerate(
-            ((w_one_hbm, w_one), (w_two_hbm, w_two), (d_one_hbm, d_one), (d_two_hbm, d_two))
+    barrier = pltpu.get_barrier_semaphore()
+
+    to_all(
+        lambda target, slot: pl.semaphore_signal(
+            barrier, inc=1, device_id=target, device_id_type=MESH
         )
+    )
+
+    wide_w = ((w_one_hbm, w_one), (w_two_hbm, w_two))
+    loads = []
+    for i, (src, dst) in enumerate(wide_w):
+        dst[3 * 384 : 4 * 384, 0:128] = jnp.zeros((384, 128), BF16)
+        dst[0:384, 128:256] = jnp.zeros((384, 128), BF16)
+        loads.append(
+            [
+                pltpu.make_async_copy(
+                    src,
+                    dst.at[p * 384 : p * 384 + 9 * REG, p * 128 : (p + 1) * 128],
+                    w_sem.at[i * 2 + p],
+                )
+                for p in range(2)
+            ]
+        )
+    loads.append([pltpu.make_async_copy(d_one_hbm, d_one, w_sem.at[4])])
+    loads.append([pltpu.make_async_copy(d_two_hbm, d_two, w_sem.at[5])])
+    near = [
+        pltpu.make_async_copy(coarse_hbm, coarse, w_sem.at[6]),
+        pltpu.make_async_copy(static_hbm, static, w_sem.at[7]),
     ]
-    for load in loads:
+    for load in near:
         load.start()
-    barrier = pltpu.get_barrier_semaphore()
-
-    def greet(step, carry):
-        pl.semaphore_signal(barrier, inc=1, device_id=partner(step), device_id_type=MESH)
-        return carry
-
-    lax.fori_loop(1, ALL, greet, 0)
-
+    for group in loads:
+        for load in group:
+            load.start()
+    for load in near:
+        load.wait()
     own32[...] = jnp.zeros_like(own32)
     for r in range(ROWS):
         own32[r * CH : r * CH + 12, 0:COLS] = coarse[:, r, :]
@@ -177,15 +227,13 @@
                 for p in range(6):
                     at = part * 384 + dx * 128 + (p + dy) * CH
                     wb_patch[at : at + CH, p * DIF : (p + 1) * DIF] = piece
-    pad32[...] = jnp.zeros_like(pad32)
+    taps[...] = jnp.zeros_like(taps)
     lane256 = lax.broadcasted_iota(jnp.int32, (1, 256), 1)
     lane128 = lax.broadcasted_iota(jnp.int32, (1, 128), 1)
     for dx in range(3):
-        base = jnp.zeros((REG, 128), F32)
         for dy in range(3):
-            pad32[0:REG, 0:OUTC] = w_out[dy * 3 + dx].astype(F32)
-            base = base + pltpu.roll(pad32[0:REG, :], (2 - dy) * CH, axis=1)
-        base = jnp.concatenate([base, jnp.zeros((REG, 128), F32)], axis=1)
+            taps[(2 - dy) * CH : (2 - dy) * CH + OUTC, 0:REG] = w_out[dy * 3 + dx].astype(F32)
+        base = jnp.concatenate([taps[:, 0:REG].T, jnp.zeros((REG, 128), F32)], axis=1)
         for e in range(3, 21):
             moved = pltpu.roll(base, ((e - 5) * CH) % 256, axis=1)
             if e < 5:
@@ -194,10 +242,9 @@
                 moved = jnp.where(lane256 >= (e - 5) * CH, moved, 0.0)
             wb_mean[(e - 3) * REG : (e - 2) * REG, dx * 256 : (dx + 1) * 256] = moved.astype(BF16)
     for dx in range(3):
-        base = jnp.zeros((DIF, 128), F32)
         for dy in range(3):
-            pad32[:, 0:OUTC] = d_out[dy * 3 + dx].astype(F32)
-            base = base + pltpu.roll(pad32[...], (2 - dy) * CH, axis=1)
+            taps[(2 - dy) * CH : (2 - dy) * CH + OUTC, :] = d_out[dy * 3 + dx].astype(F32)
+        base = taps[...].T
         for e in range(7, 17):
             moved = pltpu.roll(base, ((e - 9) * CH) % 128, axis=1)
             if e < 9:
@@ -324,18 +371,17 @@
         stat_send[which, 0:1, :] = jnp.sum(s, axis=0, keepdims=True)
         stat_send[which, 1:2, :] = jnp.sum(q, axis=0, keepdims=True)
 
-        def one(step, carry):
+        def one(target, slot):
             pltpu.make_async_remote_copy(
                 src_ref=stat_send.at[which, pl.ds(0, 2)],
-                dst_ref=recv.at[step - 1],
+                dst_ref=recv.at[slot],
                 send_sem=st_send.at[which],
                 recv_sem=st_recv.at[which],
-                device_id=partner(step),
+                device_id=target,
                 device_id_type=MESH,
             ).start()
-            return carry
-
-        lax.fori_loop(1, ALL, one, 0)
+
+        to_all(one)
 
     def band_scale(which, recv):
         pltpu.make_async_copy(recv, recv, st_recv.at[which]).wait()
@@ -415,50 +461,61 @@
     def loop(count, body):
         lax.fori_loop(0, count, lambda i, c: (body(i), c)[1], 0)
 
-    def conv_band(weight, e, rows):
+    def conv_band(weight, e, pairs):
+        def rows_of(q, dx):
+            return [
+                act[dx, pl.ds(at_row(e + 2 * k + q - 1, W), W), :] for k in range(pairs)
+            ]
+
         lhs = jnp.concatenate(
             [
-                act[dx, pl.ds(at_row(e + dy - 1, W), rows * W), :]
-                for dy in range(3)
+                jnp.concatenate(rows_of(q, dx), axis=0)
+                for q in range(4)
                 for dx in range(3)
             ],
             axis=1,
         )
-        return jnp.dot(lhs, weight[...], preferred_element_type=F32)
+        out = jnp.dot(lhs, weight[...], preferred_element_type=F32)
+        return [
+            out[(r // 2) * W : (r // 2 + 1) * W, (r % 2) * REG : (r % 2 + 1) * REG]
+            for r in range(2 * pairs)
+        ]
 
     a, b = band_scale(0, stat_one)
     loop(10, lambda i: activate_band(first, a, b, i + 7))
-    loads[0].wait()
-
-    def second_own(i, carry):
-        s, q = carry
-        e = 8 + i
-        out = conv_band(w_one, e, 1).astype(BF16)
-        second[pl.ds(at_row(e, W), W), :] = out
+    for load in loads[0]:
+        load.wait()
+
+    s = jnp.zeros((8, REG), F32)
+    q = jnp.zeros((8, REG), F32)
+    for i, out in enumerate(conv_band(w_one, 8, 4)):
+        out = out.astype(BF16)
+        second[(8 + i) * W : (9 + i) * W, :] = out
         cell = out[SIDE : SIDE + COLS].astype(F32)
-        return s + fold(cell), q + fold(cell * cell)
-
-    zero = jnp.zeros((8, REG), F32)
-    s, q = lax.fori_loop(0, ROWS, second_own, (zero, zero))
+        s = s + fold(cell)
+        q = q + fold(cell * cell)
     send_band(1, s, q, stat_two)
 
     def second_rest(i):
-        e = 2 + i + (i // 6) * 8
-        second[pl.ds(at_row(e, W), W), :] = conv_band(w_one, e, 1).astype(BF16)
+        e = 2 + i * 14
+        for k, out in enumerate(conv_band(w_one, e, 3)):
+            second[pl.ds(at_row(e + k, W), W), :] = out.astype(BF16)
 
     loop(12, lambda i: activate_band(first, a, b, 1 + i + (i // 6) * 10))
-    loop(12, second_rest)
+    loop(2, second_rest)
 
     a2, b2 = band_scale(1, stat_two)
     loop(14, lambda i: activate_band(second, a2, b2, i + 5))
-    loads[1].wait()
-
-    def third_row(e):
-        at = at_row(e, W)
-        out = first[pl.ds(at, W), :].astype(F32) + conv_band(w_two, e, 1)
-        third[pl.ds(at, W), :] = (out * row_ok(e)).astype(BF16)
-
-    loop(12, lambda i: third_row(i + 6))
+    for load in loads[1]:
+        load.wait()
+
+    def third_rows(e, pairs):
+        for k, out in enumerate(conv_band(w_two, e, pairs)):
+            at = at_row(e + k, W)
+            out = first[pl.ds(at, W), :].astype(F32) + out
+            third[pl.ds(at, W), :] = (out * row_ok(e + k)).astype(BF16)
+
+    loop(2, lambda i: third_rows(6 + 6 * i, 3))
 
     def mean_terms(low, high):
         lhs = jnp.concatenate([third[e * W : (e + 1) * W, :] for e in range(low, high)], axis=1)
@@ -511,7 +568,7 @@
         activate_band(second, a2, b2, 2 + i + (i // 3) * 14)
 
     loop(6, activate_rest)
-    loop(6, lambda i: third_row(3 + i + (i // 3) * 12))
+    loop(2, lambda i: third_rows(3 + 14 * i, 2))
     for low, high in ((3, 6), (18, 21)):
         for dx, term in enumerate(mean_terms(low, high)):
             mean_acc[dx] = mean_acc[dx] + term
@@ -538,10 +595,10 @@
         for dx in range(3):
             p_act[dx, pl.ds(at, PATCH), :] = shift(out, dx).astype(BF16)
 
-    def conv_patch(weight, e):
+    def conv_patch(weight, e, rows):
         lhs = jnp.concatenate(
             [
-                p_act[dx, pl.ds(at_row(e + dy - 6, PATCH), PATCH), :]
+                p_act[dx, pl.ds(at_row(e + dy - 6, PATCH), rows * PATCH), :]
                 for dy in range(3)
                 for dx in range(3)
             ],
@@ -551,37 +608,43 @@
 
     a3, b3 = patch_scale(2, stat_three)
     loop(10, lambda i: activate_patch(p_first, 5, a3, b3, i + 7))
-    loads[2].wait()
+    for load in loads[2]:
+        load.wait()
 
     def p_second_own(i, carry):
         s, q = carry
-        e = 8 + i
-        out = conv_patch(d_one, e).astype(BF16)
-        p_second[pl.ds(at_row(e - 6, PATCH), PATCH), :] = out
+        e = 8 + 4 * i
+        out = conv_patch(d_one, e, 4).astype(BF16)
+        p_second[pl.ds(at_row(e - 6, PATCH), 4 * PATCH), :] = out
         cell = out.astype(F32)
         return s + fold(cell), q + fold(cell * cell)
 
     zero = jnp.zeros((8, DIF), F32)
-    s, q = lax.fori_loop(0, ROWS, p_second_own, (zero, zero))
+    s, q = lax.fori_loop(0, 2, p_second_own, (zero, zero))
     send_patch(3, s, q, stat_four)
 
     def p_second_rest(i):
-        e = 6 + i + (i // 2) * 8
-        p_second[pl.ds(at_row(e - 6, PATCH), PATCH), :] = conv_patch(d_one, e).astype(BF16)
+        e = 6 + i * 10
+        out = conv_patch(d_one, e, 2).astype(BF16)
+        p_second[pl.ds(at_row(e - 6, PATCH), 2 * PATCH), :] = out
 
     loop(4, lambda i: activate_patch(p_first, 5, a3, b3, 5 + i + (i // 2) * 10))
-    loop(4, p_second_rest)
+    loop(2, p_second_rest)
 
     a4, b4 = patch_scale(3, stat_four)
     loop(12, lambda i: activate_patch(p_second, 6, a4, b4, i + 6))
-    loads[3].wait()
-
-    def p_third_row(i):
-        e = 7 + i
-        out = p_first[pl.ds(at_row(e - 5, PATCH), PATCH), :].astype(F32) + conv_patch(d_two, e)
-        p_third[pl.ds(at_row(e - 7, PATCH), PATCH), :] = (out * row_ok(e)).astype(BF16)
-
-    loop(10, p_third_row)
+    for load in loads[3]:
+        load.wait()
+
+    def p_third_rows(i):
+        e = 7 + 5 * i
+        conv = conv_patch(d_two, e, 5)
+        for k in range(5):
+            out = p_first[pl.ds(at_row(e + k - 5, PATCH), PATCH), :].astype(F32)
+            out = (out + conv[k * PATCH : (k + 1) * PATCH]) * row_ok(e + k)
+            p_third[pl.ds(at_row(e + k - 7, PATCH), PATCH), :] = out.astype(BF16)
+
+    loop(2, p_third_rows)
 
     lhs = jnp.concatenate([p_third[e * PATCH : (e + 1) * PATCH, :] for e in range(10)], axis=1)
     out = jnp.dot(lhs, wb_vel[...], preferred_element_type=F32)
@@ -622,19 +685,26 @@
     put_out(field_out, pad32[...] + total)
 
 
+def hand_over(mean_in, field_in, mean_out, field_out):
+    mean_out[...] = mean_in[...]
+    field_out[...] = field_in[...]
+
+
 def on_device(coarse, static, noise_seeds, w_in, w_one, w_two, w_out, d_in, d_one, d_two, d_out):
     vmem = pl.BlockSpec(memory_space=pltpu.VMEM)
     smem = pl.BlockSpec(memory_space=pltpu.SMEM)
     hbm = pl.BlockSpec(memory_space=pl.ANY)
     out = jax.ShapeDtypeStruct((OUTC, ROWS, COLS), F32)
-    return pl.pallas_call(
+    results = pl.pallas_call(
         kernel,
         out_shape=(out, out),
-        in_specs=[vmem, vmem, smem, vmem, hbm, hbm, vmem, vmem, hbm, hbm, vmem],
+        in_specs=[hbm, hbm, smem, vmem, hbm, hbm, vmem, vmem, hbm, hbm, vmem],
         out_specs=(vmem, vmem),
         scratch_shapes=[
-            pltpu.VMEM((9 * REG, REG), BF16),
-            pltpu.VMEM((9 * REG, REG), BF16),
+            pltpu.VMEM((OUTC, ROWS, COLS), F32),
+            pltpu.VMEM((CH - OUTC, ROWS, COLS), F32),
+            pltpu.VMEM((12 * REG, 2 * REG), BF16),
+            pltpu.VMEM((12 * REG, 2 * REG), BF16),
             pltpu.VMEM((9 * DIF, DIF), BF16),
             pltpu.VMEM((9 * DIF, DIF), BF16),
             pltpu.VMEM((128, 256), F32),
@@ -659,6 +729,7 @@
             pltpu.VMEM((10 * PATCH, DIF), BF16),
             pltpu.VMEM((3, 14 * PATCH, DIF), BF16),
             pltpu.VMEM((256, 128), F32),
+            pltpu.VMEM((128, DIF), F32),
             pltpu.VMEM((2, MARGIN, 128), F32),
             pltpu.VMEM((2, MARGIN, 128), F32),
             pltpu.VMEM((8, 8, 128), F32),
@@ -666,7 +737,7 @@
             pltpu.VMEM((ALL - 1, 2, 128), F32),
             pltpu.VMEM((LAT - 1, 4, 128), F32),
             pltpu.VMEM((LAT - 1, 4, 128), F32),
-            pltpu.SemaphoreType.DMA((4,)),
+            pltpu.SemaphoreType.DMA((8,)),
             pltpu.SemaphoreType.DMA((8,)),
             pltpu.SemaphoreType.DMA((8,)),
             pltpu.SemaphoreType.DMA((4,)),
@@ -684,12 +755,18 @@
         w_in.reshape(9, CH, REG),
         w_one.reshape(9 * REG, REG),
         w_two.reshape(9 * REG, REG),
-        w_out.reshape(9, REG, OUTC),
+        jnp.transpose(w_out.reshape(9, REG, OUTC), (0, 2, 1)),
         d_in.reshape(9, 40, DIF),
         d_one.reshape(9 * DIF, DIF),
         d_two.reshape(9 * DIF, DIF),
-        d_out.reshape(9, DIF, OUTC),
+        jnp.transpose(d_out.reshape(9, DIF, OUTC), (0, 2, 1)),
     )
+    return pl.pallas_call(
+        hand_over,
+        out_shape=(out, out),
+        in_specs=[vmem, vmem],
+        out_specs=(vmem, vmem),
+    )(*results)
 
 
 def solution(mesh):

time: 78.3 us -> 60.9 us (0.78)
  Pallas kernels: 70.1 us -> 60.1 us
  local copies, waits for them, and re-layouts: 6.75 us -> 0 us
    pallas_call x1 -> x2, Pallas kernels: 70.1 us -> 60.1 us  [the longest x1 58.5 us: on_device(): pl.pallas_call(kernel, out_shape=(out, out), in_specs=[hbm, hbm, smem, vm...]
    unnamed x4 -> x0, local copies, waits for them, and re-layouts: 6.75 us -> none
where the time goes in v1:
time: 60.9 us; the launch traced here: 60.8 us
  Pallas kernels  60.1 us (99%)
  between operations  0.64 us (1%)
    pallas_call x1, Pallas kernels, on_device(): pl.pallas_call(kernel, out_shape=(out, out), in_specs=[hbm, hbm, smem, vm...  58.5 us
    pallas_call x1, Pallas kernels, on_device(): pl.pallas_call(hand_over, out_shape=(out, out), in_specs=[vmem, vmem], ou...  1.62 us

profile of v1, /device:TPU:1, one launch (start us, length us, event | category | flops | bytes accessed | tf_op | source)
XLA Modules:
  0.0 60.8 jit_solution(12532219518219204245)
XLA Ops:
  0.6 58.5 %shard_map.122 = (f32[12,8,192]{2,1,0:T(8,128)}, f32[12,8,192]{2,1,0:T(8,128)}) custom-call(f32[12,8,192]{2,1,0:T(8,128)} %coarse_hbm.1, f32[4,8,192]{2,1,0:T(8,128)} %static_hbm.1, s32[64]{0:T(128)} %seeds.1, bf16[9,16,128]{2,1,0:T(8,128)(2,1)} %bitcast.18, bf16[1152,128]{1,0:T(8,128)(2,1)} %bitcast.14, bf16[1152,128]{1,0:T(8,128)(2,1)} %bitcast.15, ...), custom_call_target="tpu_custom_call" | custom-call | tf_op jit(solution)/shard_map/pallas_call | solution.py:698
  59.2 1.6 %shard_map.123 = (f32[12,8,192]{2,1,0:T(8,128)}, f32[12,8,192]{2,1,0:T(8,128)}) custom-call(f32[12,8,192]{2,1,0:T(8,128)} %get-tuple-element.4.mean_in, f32[12,8,192]{2,1,0:T(8,128)} %get-tuple-element.5.field_in), custom_call_target="tpu_custom_call" | custom-call | tf_op jit(solution)/shard_map/pallas_call | solution.py:764

commit v2 on v1

--- a/solution.py
+++ b/solution.py
@@ -28,6 +28,10 @@
 DIF = 256
 OUTC = 12
 STEPS = (2, 1, 3, 0)
+P_SECOND_GROUPS = ((8, 4), (12, 4))
+P_THIRD_GROUPS = ((7, 4), (11, 4), (15, 2))
+SECOND_GROUPS = ((8, 2), (12, 2))
+THIRD_GROUPS = ((6, 2), (10, 2), (14, 2))
 EPS = 1e-05
 
 AROUND = ((0, -1), (0, 1), (-1, -1), (-1, 0), (-1, 1), (1, -1), (1, 0), (1, 1))
@@ -41,7 +45,7 @@
 
 
 def at_row(row, width):
-    return pl.multiple_of(row * width, 16)
+    return row * width if isinstance(row, int) else pl.multiple_of(row * width, 16)
 
 
 def all_groups(stats, size):
@@ -73,18 +77,22 @@
     coarse_hbm,
     static_hbm,
     seeds,
-    w_in,
+    w_in_hbm,
     w_one_hbm,
     w_two_hbm,
-    w_out,
-    d_in,
+    w_out_hbm,
+    d_in_hbm,
     d_one_hbm,
     d_two_hbm,
-    d_out,
+    d_out_hbm,
     mean_out,
     field_out,
     coarse,
     static,
+    w_in,
+    w_out,
+    d_in,
+    d_out,
     w_one,
     w_two,
     d_one,
@@ -193,6 +201,10 @@
     near = [
         pltpu.make_async_copy(coarse_hbm, coarse, w_sem.at[6]),
         pltpu.make_async_copy(static_hbm, static, w_sem.at[7]),
+        pltpu.make_async_copy(w_in_hbm, w_in, w_sem.at[8]),
+        pltpu.make_async_copy(w_out_hbm, w_out, w_sem.at[9]),
+        pltpu.make_async_copy(d_in_hbm, d_in, w_sem.at[10]),
+        pltpu.make_async_copy(d_out_hbm, d_out, w_sem.at[11]),
     ]
     for load in near:
         load.start()
@@ -271,13 +283,21 @@
             return jnp.where(spot == count - 1, 0.0, pltpu.roll(values, count - 1, axis=0))
         return values
 
+    spot_low = lax.broadcasted_iota(jnp.int32, (16, 128), 0)
+
     def put_part(part, values):
-        for dx in range(3):
-            moved = shift(values, dx)
-            at = part * 384 + dx * 128
-            parts[0, :, at : at + 128] = moved[:, :128].astype(BF16)
-            parts[1, :, at : at + 128] = pltpu.roll(moved, 192, axis=1)[:, :128].astype(BF16)
-            parts[2, :, at : at + 128] = moved[:, 128:].astype(BF16)
+        windows = (values[:, :128], pltpu.roll(values, 192, axis=1)[:, :128], values[:, 128:])
+        for win, block in enumerate(windows):
+            at = part * 384
+            later = pltpu.roll(block, 1, axis=0)
+            sooner = pltpu.roll(block, PATCH - 1, axis=0)
+            parts[win, 0:16, at : at + 128] = jnp.where(spot_low == 0, 0.0, later[:16]).astype(BF16)
+            parts[win, 16:, at : at + 128] = later[16:].astype(BF16)
+            parts[win, :, at + 128 : at + 256] = block.astype(BF16)
+            parts[win, :-16, at + 256 : at + 384] = sooner[:-16].astype(BF16)
+            parts[win, PATCH - 16 :, at + 256 : at + 384] = jnp.where(
+                spot_low == 15, 0.0, sooner[-16:]
+            ).astype(BF16)
 
     def noise_rows(i, carry):
         at = pl.multiple_of(i * 32, 32)
@@ -324,13 +344,19 @@
         copies[k].wait_recv()
 
     def assemble(centre, left, right):
-        lane = lax.broadcasted_iota(jnp.int32, (128, 384), 1)
-        zeros = jnp.zeros((128, 128), F32)
-        mid = pltpu.roll(jnp.concatenate([centre, zeros], axis=1), SIDE, axis=1)
-        low = pltpu.roll(jnp.concatenate([left, zeros, zeros], axis=1), 384 - 24, axis=1)
-        high = pltpu.roll(jnp.concatenate([right, zeros, zeros], axis=1), SIDE + COLS, axis=1)
-        inner = jnp.where(lane < SIDE + COLS, mid, jnp.where(lane < W, high, 0.0))
-        return jnp.where(lane < SIDE, low, inner)
+        lane = lax.broadcasted_iota(jnp.int32, (128, 128), 1)
+        low = pltpu.roll(left, 128 - 24, axis=1)
+        one = pltpu.roll(centre[:, :128], SIDE, axis=1)
+        two = pltpu.roll(centre[:, 128:], SIDE, axis=1)
+        high = pltpu.roll(right, SIDE + COLS - 128, axis=1)
+        return jnp.concatenate(
+            [
+                jnp.where(lane < SIDE, low, one),
+                jnp.where(lane < SIDE, one, jnp.where(lane < SIDE + COLS - 128, two, high)),
+                jnp.where(lane < W - 256, high, 0.0),
+            ],
+            axis=1,
+        )
 
     up = assemble(tall[1].astype(F32), wide[7 - 2].astype(F32), wide[4 - 2].astype(F32))
     mid = assemble(own16[...].astype(F32), wide[6 - 2].astype(F32), wide[3 - 2].astype(F32))
@@ -339,17 +365,16 @@
     down = jnp.where(lat == LAT - 1, 0.0, down)
     xt = jnp.concatenate([up.T, mid.T, down.T], axis=1)[:W]
     xt_far = pltpu.roll(xt, 320, axis=1)
-    for dx in range(3):
-        if dx == 0:
-            near, far = pltpu.roll(xt, 1, axis=0), pltpu.roll(xt_far, 1, axis=0)
-        elif dx == 2:
-            near, far = pltpu.roll(xt, W - 1, axis=0), pltpu.roll(xt_far, W - 1, axis=0)
-        else:
-            near, far = xt, xt_far
-        for win in range(5):
-            source = (near, far)[win % 2]
-            at = (win // 2) * 128
-            xw[win, :, dx * 128 : (dx + 1) * 128] = source[:, at : at + 128].astype(BF16)
+
+    def put_window(win):
+        at = (win // 2) * 128
+        block = (xt, xt_far)[win % 2][:, at : at + 128]
+        xw[win, :, 0:128] = pltpu.roll(block, 1, axis=0).astype(BF16)
+        xw[win, :, 128:256] = block.astype(BF16)
+        xw[win, :, 256:384] = pltpu.roll(block, W - 1, axis=0).astype(BF16)
+
+    for win in (1, 2, 3):
+        put_window(win)
 
     def first_rows(win, low, high):
         out = jnp.dot(
@@ -420,6 +445,8 @@
     stat_send[...] = jnp.zeros_like(stat_send)
     send_band(0, sum(s for s, _ in stats), sum(q for _, q in stats), stat_one)
 
+    put_window(0)
+    put_window(4)
     first_rows(0, 0, 6)
     first_rows(1, 2, 3)
     first_rows(3, 3, 6)
@@ -482,18 +509,21 @@
         ]
 
     a, b = band_scale(0, stat_one)
-    loop(10, lambda i: activate_band(first, a, b, i + 7))
     for load in loads[0]:
         load.wait()
-
     s = jnp.zeros((8, REG), F32)
     q = jnp.zeros((8, REG), F32)
-    for i, out in enumerate(conv_band(w_one, 8, 4)):
-        out = out.astype(BF16)
-        second[(8 + i) * W : (9 + i) * W, :] = out
-        cell = out[SIDE : SIDE + COLS].astype(F32)
-        s = s + fold(cell)
-        q = q + fold(cell * cell)
+    ready = 7
+    for e, pairs in SECOND_GROUPS:
+        while ready <= e + 2 * pairs:
+            activate_band(first, a, b, ready)
+            ready += 1
+        for i, out in enumerate(conv_band(w_one, e, pairs)):
+            out = out.astype(BF16)
+            second[(e + i) * W : (e + i + 1) * W, :] = out
+            cell = out[SIDE : SIDE + COLS].astype(F32)
+            s = s + fold(cell)
+            q = q + fold(cell * cell)
     send_band(1, s, q, stat_two)
 
     def second_rest(i):
@@ -505,7 +535,6 @@
     loop(2, second_rest)
 
     a2, b2 = band_scale(1, stat_two)
-    loop(14, lambda i: activate_band(second, a2, b2, i + 5))
     for load in loads[1]:
         load.wait()
 
@@ -515,7 +544,12 @@
             out = first[pl.ds(at, W), :].astype(F32) + out
             third[pl.ds(at, W), :] = (out * row_ok(e + k)).astype(BF16)
 
-    loop(2, lambda i: third_rows(6 + 6 * i, 3))
+    ready = 5
+    for e, pairs in THIRD_GROUPS:
+        while ready <= e + 2 * pairs:
+            activate_band(second, a2, b2, ready)
+            ready += 1
+        third_rows(e, pairs)
 
     def mean_terms(low, high):
         lhs = jnp.concatenate([third[e * W : (e + 1) * W, :] for e in range(low, high)], axis=1)
@@ -587,13 +621,22 @@
     patch_first_rows(0, rest_rows(0))
     patch_first_rows(2, rest_rows(2))
 
+    spot16 = lax.broadcasted_iota(jnp.int32, (16, DIF), 0)
+
     def activate_patch(source, shift_row, a, b, e):
         ok = row_ok(e)
         half = source[pl.ds(at_row(e - shift_row, PATCH), PATCH), :].astype(F32) * (a * ok) + b * ok
         out = half_silu(half)
         at = at_row(e - 5, PATCH)
-        for dx in range(3):
-            p_act[dx, pl.ds(at, PATCH), :] = shift(out, dx).astype(BF16)
+        later = pltpu.roll(out, 1, axis=0)
+        sooner = pltpu.roll(out, PATCH - 1, axis=0)
+        p_act[0, pl.ds(at, 16), :] = jnp.where(spot16 == 0, 0.0, later[:16]).astype(BF16)
+        p_act[0, pl.ds(at + 16, PATCH - 16), :] = later[16:].astype(BF16)
+        p_act[1, pl.ds(at, PATCH), :] = out.astype(BF16)
+        p_act[2, pl.ds(at, PATCH - 16), :] = sooner[:-16].astype(BF16)
+        p_act[2, pl.ds(at + PATCH - 16, 16), :] = jnp.where(
+            spot16 == 15, 0.0, sooner[-16:]
+        ).astype(BF16)
 
     def conv_patch(weight, e, rows):
         lhs = jnp.concatenate(
@@ -607,20 +650,20 @@
         return jnp.dot(lhs, weight[...], preferred_element_type=F32)
 
     a3, b3 = patch_scale(2, stat_three)
-    loop(10, lambda i: activate_patch(p_first, 5, a3, b3, i + 7))
     for load in loads[2]:
         load.wait()
-
-    def p_second_own(i, carry):
-        s, q = carry
-        e = 8 + 4 * i
-        out = conv_patch(d_one, e, 4).astype(BF16)
-        p_second[pl.ds(at_row(e - 6, PATCH), 4 * PATCH), :] = out
+    s = jnp.zeros((8, DIF), F32)
+    q = jnp.zeros((8, DIF), F32)
+    ready = 7
+    for e, rows in P_SECOND_GROUPS:
+        while ready <= e + rows:
+            activate_patch(p_first, 5, a3, b3, ready)
+            ready += 1
+        out = conv_patch(d_one, e, rows).astype(BF16)
+        p_second[(e - 6) * PATCH : (e - 6 + rows) * PATCH, :] = out
         cell = out.astype(F32)
-        return s + fold(cell), q + fold(cell * cell)
-
-    zero = jnp.zeros((8, DIF), F32)
-    s, q = lax.fori_loop(0, 2, p_second_own, (zero, zero))
+        s = s + fold(cell)
+        q = q + fold(cell * cell)
     send_patch(3, s, q, stat_four)
 
     def p_second_rest(i):
@@ -632,19 +675,18 @@
     loop(2, p_second_rest)
 
     a4, b4 = patch_scale(3, stat_four)
-    loop(12, lambda i: activate_patch(p_second, 6, a4, b4, i + 6))
     for load in loads[3]:
         load.wait()
-
-    def p_third_rows(i):
-        e = 7 + 5 * i
-        conv = conv_patch(d_two, e, 5)
-        for k in range(5):
-            out = p_first[pl.ds(at_row(e + k - 5, PATCH), PATCH), :].astype(F32)
+    ready = 6
+    for e, rows in P_THIRD_GROUPS:
+        while ready <= e + rows:
+            activate_patch(p_second, 6, a4, b4, ready)
+            ready += 1
+        conv = conv_patch(d_two, e, rows)
+        for k in range(rows):
+            out = p_first[(e + k - 5) * PATCH : (e + k - 4) * PATCH, :].astype(F32)
             out = (out + conv[k * PATCH : (k + 1) * PATCH]) * row_ok(e + k)
-            p_third[pl.ds(at_row(e + k - 7, PATCH), PATCH), :] = out.astype(BF16)
-
-    loop(2, p_third_rows)
+            p_third[(e + k - 7) * PATCH : (e + k - 6) * PATCH, :] = out.astype(BF16)
 
     lhs = jnp.concatenate([p_third[e * PATCH : (e + 1) * PATCH, :] for e in range(10)], axis=1)
     out = jnp.dot(lhs, wb_vel[...], preferred_element_type=F32)
@@ -697,12 +739,16 @@
     out = jax.ShapeDtypeStruct((OUTC, ROWS, COLS), F32)
     results = pl.pallas_call(
         kernel,
-        out_shape=(out, out),
-        in_specs=[hbm, hbm, smem, vmem, hbm, hbm, vmem, vmem, hbm, hbm, vmem],
+        out_shape=(pltpu.VMEM((OUTC, ROWS, COLS), F32),) * 2,
+        in_specs=[hbm, hbm, smem] + [hbm] * 8,
         out_specs=(vmem, vmem),
         scratch_shapes=[
             pltpu.VMEM((OUTC, ROWS, COLS), F32),
             pltpu.VMEM((CH - OUTC, ROWS, COLS), F32),
+            pltpu.VMEM((9, CH, REG), BF16),
+            pltpu.VMEM((9, OUTC, REG), BF16),
+            pltpu.VMEM((9, 40, DIF), BF16),
+            pltpu.VMEM((9, OUTC, DIF), BF16),
             pltpu.VMEM((12 * REG, 2 * REG), BF16),
             pltpu.VMEM((12 * REG, 2 * REG), BF16),
             pltpu.VMEM((9 * DIF, DIF), BF16),
@@ -737,7 +783,7 @@
             pltpu.VMEM((ALL - 1, 2, 128), F32),
             pltpu.VMEM((LAT - 1, 4, 128), F32),
             pltpu.VMEM((LAT - 1, 4, 128), F32),
-            pltpu.SemaphoreType.DMA((8,)),
+            pltpu.SemaphoreType.DMA((12,)),
             pltpu.SemaphoreType.DMA((8,)),
             pltpu.SemaphoreType.DMA((8,)),
             pltpu.SemaphoreType.DMA((4,)),
@@ -766,6 +812,7 @@
         out_shape=(out, out),
         in_specs=[vmem, vmem],
         out_specs=(vmem, vmem),
+        compiler_params=pltpu.CompilerParams(vmem_limit_bytes=4 * 1024 * 1024),
     )(*results)
 
 

time: 60.9 us -> 56.5 us (0.928)
  Pallas kernels: 60.1 us -> 55.7 us
    pallas_call x1, Pallas kernels: 58.5 us -> 55 us  [on_device(): pl.pallas_call(kernel, out_shape=(pltpu.VMEM((OUTC, ROWS, COLS), F32),) *...]
    pallas_call x1, Pallas kernels: 1.62 us -> 0.69 us  [on_device(): pl.pallas_call(hand_over, out_shape=(out, out), in_specs=[vmem, vmem], ou...]
where the time goes in v2:
time: 56.5 us; the launch traced here: 56.4 us
  Pallas kernels  55.7 us (99%)
  between operations  0.64 us (1%)
    pallas_call x1, Pallas kernels, on_device(): pl.pallas_call(kernel, out_shape=(pltpu.VMEM((OUTC, ROWS, COLS), F32),) *...  55 us

profile of v2, /device:TPU:1, one launch (start us, length us, event | category | flops | bytes accessed | tf_op | source)
XLA Modules:
  0.0 56.4 jit_solution(11086651150839064206)
XLA Ops:
  0.6 55.0 %shard_map.122 = (f32[12,8,192]{2,1,0:T(8,128)S(1)}, f32[12,8,192]{2,1,0:T(8,128)S(1)}) custom-call(f32[12,8,192]{2,1,0:T(8,128)} %coarse_hbm.1, f32[4,8,192]{2,1,0:T(8,128)} %static_hbm.1, s32[64]{0:T(128)} %seeds.1, bf16[9,16,128]{2,1,0:T(8,128)(2,1)} %bitcast.18, bf16[1152,128]{1,0:T(8,128)(2,1)} %bitcast.14, bf16[1152,128]{1,0:T(8,128)(2,1)} %bitcast.15, ...), custom_call_target="tpu_custom_call" | custom-call | tf_op jit(solution)/shard_map/pallas_call | solution.py:740
  55.7 0.7 %shard_map.123 = (f32[12,8,192]{2,1,0:T(8,128)}, f32[12,8,192]{2,1,0:T(8,128)}) custom-call(f32[12,8,192]{2,1,0:T(8,128)S(1)} %get-tuple-element.4.mean_in, f32[12,8,192]{2,1,0:T(8,128)S(1)} %get-tuple-element.5.field_in), custom_call_target="tpu_custom_call" | custom-call | tf_op jit(solution)/shard_map/pallas_call | solution.py:810

commit v3 on v2

--- a/solution.py
+++ b/solution.py
@@ -104,6 +104,7 @@
     xw,
     wb_in,
     wb_patch,
+    wb_mix,
     wb_mean,
     wb_vel,
     first,
@@ -112,8 +113,9 @@
     act,
     noise_keep,
     parts,
+    mixed,
     partial,
-    mean_acc,
+    mean_keep,
     p_first,
     p_second,
     p_third,
@@ -226,15 +228,16 @@
                 at = dx * 128 + (p + dy) * CH
                 wb_in[at : at + CH, p * REG : (p + 1) * REG] = w_in[dy * 3 + dx]
     wb_patch[...] = jnp.zeros_like(wb_patch)
+    wb_mix[...] = jnp.zeros_like(wb_mix)
     low_rows = lax.broadcasted_iota(jnp.int32, (40, DIF), 0) < OUTC
     for dy in range(3):
         for dx in range(3):
             raw = d_in[dy * 3 + dx].astype(F32)
-            pieces = (
-                jnp.where(low_rows, raw, 0.0)[:CH].astype(BF16),
-                raw[24:40].astype(BF16),
-                jnp.where(low_rows, pltpu.roll(raw, 28, axis=0), 0.0)[:CH].astype(BF16),
-            )
+            pieces = (jnp.where(low_rows, raw, 0.0)[:CH].astype(BF16), raw[24:40].astype(BF16))
+            mean_piece = jnp.where(low_rows, pltpu.roll(raw, 28, axis=0), 0.0)[:CH].astype(BF16)
+            for p in range(2):
+                at = dx * 64 + (p + dy) * CH
+                wb_mix[at : at + CH, p * DIF : (p + 1) * DIF] = mean_piece
             for part, piece in enumerate(pieces):
                 for p in range(6):
                     at = part * 384 + dx * 128 + (p + dy) * CH
@@ -242,28 +245,25 @@
     taps[...] = jnp.zeros_like(taps)
     lane256 = lax.broadcasted_iota(jnp.int32, (1, 256), 1)
     lane128 = lax.broadcasted_iota(jnp.int32, (1, 128), 1)
-    for dx in range(3):
-        for dy in range(3):
-            taps[(2 - dy) * CH : (2 - dy) * CH + OUTC, 0:REG] = w_out[dy * 3 + dx].astype(F32)
-        base = jnp.concatenate([taps[:, 0:REG].T, jnp.zeros((REG, 128), F32)], axis=1)
-        for e in range(3, 21):
-            moved = pltpu.roll(base, ((e - 5) * CH) % 256, axis=1)
-            if e < 5:
-                moved = jnp.where(lane256 < (e - 2) * CH, moved, 0.0)
-            if e > 18:
-                moved = jnp.where(lane256 >= (e - 5) * CH, moved, 0.0)
-            wb_mean[(e - 3) * REG : (e - 2) * REG, dx * 256 : (dx + 1) * 256] = moved.astype(BF16)
-    for dx in range(3):
-        for dy in range(3):
-            taps[(2 - dy) * CH : (2 - dy) * CH + OUTC, :] = d_out[dy * 3 + dx].astype(F32)
-        base = taps[...].T
-        for e in range(7, 17):
-            moved = pltpu.roll(base, ((e - 9) * CH) % 128, axis=1)
-            if e < 9:
-                moved = jnp.where(lane128 < (e - 6) * CH, moved, 0.0)
-            if e > 14:
-                moved = jnp.where(lane128 >= (e - 9) * CH, moved, 0.0)
-            wb_vel[(e - 7) * DIF : (e - 6) * DIF, dx * 128 : (dx + 1) * 128] = moved.astype(BF16)
+    half_lane = lane128 < 64
+
+    def out_weights(weight, depth, bank):
+        bases = []
+        for dx in range(3):
+            for dy in range(3):
+                at = (2 - dy) * CH
+                taps[at : at + OUTC, 0:depth] = weight[dy * 3 + dx].astype(F32)
+            bases.append(taps[:, 0:depth].T)
+        for i in range(6):
+            step = ((i - 2) * CH) % 128
+            zero, one, two = (pltpu.roll(base, step, axis=1) for base in bases)
+            rows = slice(i * depth, (i + 1) * depth)
+            one = pltpu.roll(one, 64, axis=1)
+            bank[rows, 0:128] = jnp.where(half_lane, zero, one).astype(BF16)
+            bank[rows, 128:256] = jnp.where(half_lane, two, 0.0).astype(BF16)
+
+    out_weights(w_out, REG, wb_mean)
+    out_weights(d_out, DIF, wb_vel)
 
     lane_row = lane256 // CH
     lane_ok = jnp.zeros((1, 256), F32)
@@ -551,63 +551,79 @@
             ready += 1
         third_rows(e, pairs)
 
-    def mean_terms(low, high):
-        lhs = jnp.concatenate([third[e * W : (e + 1) * W, :] for e in range(low, high)], axis=1)
-        return [
-            jnp.dot(
-                lhs,
-                wb_mean[(low - 3) * REG : (high - 3) * REG, dx * 256 : (dx + 1) * 256],
-                preferred_element_type=F32,
+    def mean_windows(starts):
+        lhs = jnp.concatenate(
+            [
+                jnp.concatenate([third[(e + i - 1) * W : (e + i) * W, :] for e in starts], axis=0)
+                for i in range(6)
+            ],
+            axis=1,
+        )
+        out = jnp.dot(lhs, wb_mean[...], preferred_element_type=F32)
+        windows = []
+        for k, e in enumerate(starts):
+            low, high = out[k * W : (k + 1) * W, 0:128], out[k * W : (k + 1) * W, 128:256]
+            mean = (
+                pltpu.roll(low, 1, axis=0)
+                + pltpu.roll(low, 64, axis=1)
+                + pltpu.roll(high, W - 1, axis=0)
             )
-            for dx in range(3)
-        ]
-
-    def put_mean():
-        total = (
-            pltpu.roll(mean_acc[0], 1, axis=0)
-            + mean_acc[1]
-            + pltpu.roll(mean_acc[2], W - 1, axis=0)
-        )[OFF : OFF + PATCH]
-        put_part(2, total * lane_ok)
-        return total
-
-    def patch_first_rows(win, span):
-        low, high = span
-        out = jnp.dot(
-            parts[win, :, 768:1152],
-            wb_patch[768:1152, low * DIF : high * DIF],
-            preferred_element_type=F32,
-        )
+            ok = jnp.zeros((1, 128), F32)
+            for q in range(4):
+                ok = jnp.where(lane128 // CH == q, row_ok(e + q), ok)
+            windows.append(mean[OFF : OFF + PATCH] * ok)
+        return windows
+
+    def put_mixed(windows):
+        for k, mean in enumerate(windows):
+            at = k * PATCH
+            later = pltpu.roll(mean, 1, axis=0)
+            sooner = pltpu.roll(mean, PATCH - 1, axis=0)
+            low = jnp.where(half_lane, later, pltpu.roll(mean, 64, axis=1))
+            head = jnp.where((spot_low == 0) & half_lane, 0.0, low[:16])
+            tail = jnp.where(spot_low == 15, 0.0, sooner[-16:])
+            mixed[at : at + 16, 0:128] = head.astype(BF16)
+            mixed[at + 16 : at + PATCH, 0:128] = low[16:].astype(BF16)
+            mixed[at : at + PATCH - 16, 128:256] = sooner[:-16].astype(BF16)
+            mixed[at + PATCH - 16 : at + PATCH, 128:256] = tail.astype(BF16)
+
+    def patch_first_rows(starts, skip):
+        out = jnp.dot(mixed[...], wb_mix[...], preferred_element_type=F32)
         s = jnp.zeros((8, DIF), F32)
         q = jnp.zeros((8, DIF), F32)
-        for p in range(low, high):
-            e = win * 4 + 5 + p
-            at = (e - 5) * PATCH
-            row = out[:, (p - low) * DIF : (p - low + 1) * DIF] + partial[at : at + PATCH, :]
-            row = row.astype(BF16)
-            p_first[at : at + PATCH, :] = row
-            if 8 <= e < 16:
-                cell = row.astype(F32)
-                s = s + fold(cell)
-                q = q + fold(cell * cell)
+        for k, start in enumerate(starts):
+            for p in range(2):
+                e = start + 1 + p
+                if (k, p) in skip:
+                    continue
+                at = (e - 5) * PATCH
+                row = out[k * PATCH : (k + 1) * PATCH, p * DIF : (p + 1) * DIF]
+                row = (row + partial[at : at + PATCH, :]).astype(BF16)
+                p_first[at : at + PATCH, :] = row
+                if 8 <= e < 16:
+                    cell = row.astype(F32)
+                    s = s + fold(cell)
+                    q = q + fold(cell * cell)
         return s, q
 
-    for dx, term in enumerate(mean_terms(6, 18)):
-        mean_acc[dx] = term
-    put_mean()
-    stats = [patch_first_rows(win, patch_rows(win)) for win in range(3)]
-    send_patch(2, sum(s for s, _ in stats), sum(q for _, q in stats), stat_three)
+    windows = mean_windows((7, 9, 11, 13))
+    put_mixed(windows)
+    for k, mean in enumerate(windows):
+        mean_keep[k] = mean
+    s, q = patch_first_rows((7, 9, 11, 13), ())
+    send_patch(2, s, q, stat_three)
 
     def activate_rest(i):
         activate_band(second, a2, b2, 2 + i + (i // 3) * 14)
 
     loop(6, activate_rest)
     loop(2, lambda i: third_rows(3 + 14 * i, 2))
-    for low, high in ((3, 6), (18, 21)):
-        for dx, term in enumerate(mean_terms(low, high)):
-            mean_acc[dx] = mean_acc[dx] + term
-    mean_all = put_mean()
-    mean_own = pltpu.roll(mean_all, 192, axis=1)[:, :128]
+    put_mixed(mean_windows((4, 6, 15, 16)))
+    patch_first_rows((4, 6, 15, 16), ((1, 1), (3, 0)))
+    mean_own = jnp.zeros((PATCH, 128), F32)
+    for k in range(4):
+        here = lane128 // 32 == k
+        mean_own = jnp.where(here, pltpu.roll(mean_keep[k], (32 * k - CH) % 128, axis=1), mean_own)
     noise_own = pltpu.roll(noise_keep[...], 192, axis=1)[:, :128]
     base = mean_own + noise_own
 
@@ -618,8 +634,6 @@
 
     put_out(mean_out, mean_own)
     pad32[...] = base
-    patch_first_rows(0, rest_rows(0))
-    patch_first_rows(2, rest_rows(2))
 
     spot16 = lax.broadcasted_iota(jnp.int32, (16, DIF), 0)
 
@@ -688,9 +702,20 @@
             out = (out + conv[k * PATCH : (k + 1) * PATCH]) * row_ok(e + k)
             p_third[(e + k - 7) * PATCH : (e + k - 6) * PATCH, :] = out.astype(BF16)
 
-    lhs = jnp.concatenate([p_third[e * PATCH : (e + 1) * PATCH, :] for e in range(10)], axis=1)
+    lhs = jnp.concatenate(
+        [
+            jnp.concatenate([p_third[r * PATCH : (r + 1) * PATCH, :] for r in (i, i + 4)], axis=0)
+            for i in range(6)
+        ],
+        axis=1,
+    )
     out = jnp.dot(lhs, wb_vel[...], preferred_element_type=F32)
-    velocity = shift(out[:, 0:128], 0) + out[:, 128:256] + shift(out[:, 256:384], 2)
+
+    def of_window(k):
+        low, high = out[k * PATCH : (k + 1) * PATCH, :128], out[k * PATCH : (k + 1) * PATCH, 128:]
+        return shift(low, 0) + pltpu.roll(low, 64, axis=1) + shift(high, 2)
+
+    velocity = jnp.where(half_lane, of_window(0), pltpu.roll(of_window(1), 64, axis=1))
     edge_send[0] = velocity[0:MARGIN]
     edge_send[1] = velocity[PATCH - MARGIN : PATCH]
     edges = [
@@ -759,17 +784,19 @@
             pltpu.VMEM((6, 128, 128), BF16),
             pltpu.VMEM((5, W, 384), BF16),
             pltpu.VMEM((384, 6 * REG), BF16),
-            pltpu.VMEM((1152, 6 * DIF), BF16),
-            pltpu.VMEM((18 * REG, 768), BF16),
-            pltpu.VMEM((10 * DIF, 384), BF16),
+            pltpu.VMEM((768, 6 * DIF), BF16),
+            pltpu.VMEM((256, 2 * DIF), BF16),
+            pltpu.VMEM((6 * REG, 256), BF16),
+            pltpu.VMEM((6 * DIF, 256), BF16),
             pltpu.VMEM((FRAME * W, REG), BF16),
             pltpu.VMEM((FRAME * W, REG), BF16),
             pltpu.VMEM((FRAME * W, REG), BF16),
             pltpu.VMEM((3, FRAME * W, REG), BF16),
             pltpu.VMEM((PATCH, 256), F32),
-            pltpu.VMEM((3, PATCH, 1152), BF16),
+            pltpu.VMEM((3, PATCH, 768), BF16),
+            pltpu.VMEM((4 * PATCH, 256), BF16),
             pltpu.VMEM((14 * PATCH, DIF), F32),
-            pltpu.VMEM((3, W, 256), F32),
+            pltpu.VMEM((4, PATCH, 128), F32),
             pltpu.VMEM((14 * PATCH, DIF), BF16),
             pltpu.VMEM((12 * PATCH, DIF), BF16),
             pltpu.VMEM((10 * PATCH, DIF), BF16),

time: 56.5 us -> 55.1 us (0.975)
  Pallas kernels: 55.7 us -> 54.4 us
    pallas_call x1, Pallas kernels: 55 us -> 53.7 us  [on_device(): pl.pallas_call(kernel, out_shape=(pltpu.VMEM((OUTC, ROWS, COLS), F32),) *...]
where the time goes in v3:
time: 55.1 us; the launch traced here: 55 us
  Pallas kernels  54.4 us (99%)
  between operations  0.64 us (1%)
    pallas_call x1, Pallas kernels, on_device(): pl.pallas_call(kernel, out_shape=(pltpu.VMEM((OUTC, ROWS, COLS), F32),) *...  53.7 us

profile of v3, /device:TPU:1, one launch (start us, length us, event | category | flops | bytes accessed | tf_op | source)
XLA Modules:
  0.0 55.0 jit_solution(17849366530673691816)
XLA Ops:
  0.6 53.7 %shard_map.122 = (f32[12,8,192]{2,1,0:T(8,128)S(1)}, f32[12,8,192]{2,1,0:T(8,128)S(1)}) custom-call(f32[12,8,192]{2,1,0:T(8,128)} %coarse_hbm.1, f32[4,8,192]{2,1,0:T(8,128)} %static_hbm.1, s32[64]{0:T(128)} %seeds.1, bf16[9,16,128]{2,1,0:T(8,128)(2,1)} %bitcast.18, bf16[1152,128]{1,0:T(8,128)(2,1)} %bitcast.14, bf16[1152,128]{1,0:T(8,128)(2,1)} %bitcast.15, ...), custom_call_target="tpu_custom_call" | custom-call | tf_op jit(solution)/shard_map/pallas_call | solution.py:765
  54.3 0.7 %shard_map.123 = (f32[12,8,192]{2,1,0:T(8,128)}, f32[12,8,192]{2,1,0:T(8,128)}) custom-call(f32[12,8,192]{2,1,0:T(8,128)S(1)} %get-tuple-element.4.mean_in, f32[12,8,192]{2,1,0:T(8,128)S(1)} %get-tuple-element.5.field_in), custom_call_target="tpu_custom_call" | custom-call | tf_op jit(solution)/shard_map/pallas_call | solution.py:837

commit v4 on v3

--- a/solution.py
+++ b/solution.py
@@ -731,25 +731,31 @@
     ]
     for edge in edges:
         edge.start()
+    total = jnp.concatenate(
+        [
+            velocity[0:MARGIN],
+            velocity[MARGIN : 2 * MARGIN] * 0.5,
+            velocity[2 * MARGIN : COLS],
+            velocity[COLS : COLS + MARGIN] * 0.5,
+            velocity[COLS + MARGIN :],
+        ],
+        axis=0,
+    )
+    own32[...] = pltpu.roll((pad32[...] + total).T, PATCH - MARGIN, axis=1)
     for k in order:
         copies[k].wait_send()
     for which, recv in enumerate((stat_one, stat_two, stat_three, stat_four)):
         pltpu.make_async_copy(recv, recv, st_send.at[which]).wait()
     for edge in edges:
         edge.wait()
-    from_left = velocity[MARGIN : 2 * MARGIN] + edge_recv[1]
-    from_right = velocity[COLS : COLS + MARGIN] + edge_recv[0]
-    total = jnp.concatenate(
-        [
-            velocity[0:MARGIN],
-            from_left * 0.5,
-            velocity[2 * MARGIN : COLS],
-            from_right * 0.5,
-            velocity[COLS + MARGIN :],
-        ],
-        axis=0,
-    )
-    put_out(field_out, pad32[...] + total)
+    margins = jnp.concatenate(
+        [edge_recv[1], edge_recv[0], jnp.zeros((2 * MARGIN, 128), F32)], axis=0
+    ).T
+    margins = margins * 0.5
+    left = jnp.where(lane128 < MARGIN, margins, 0.0)
+    flat = own32[...] + jnp.concatenate([left, margins - left], axis=1)
+    for r in range(ROWS):
+        field_out[:, r, :] = flat[r * CH : r * CH + OUTC, :COLS]
 
 
 def hand_over(mean_in, field_in, mean_out, field_out):

time: 55.1 us -> 55 us (level)
  no operation moved by 1% of the time
where the time goes in v4:
time: 55 us; the launch traced here: 54.9 us
  Pallas kernels  54.3 us (99%)
  between operations  0.64 us (1%)
    pallas_call x1, Pallas kernels, on_device(): pl.pallas_call(kernel, out_shape=(pltpu.VMEM((OUTC, ROWS, COLS), F32),) *...  53.6 us

profile of v4, /device:TPU:1, one launch (start us, length us, event | category | flops | bytes accessed | tf_op | source)
XLA Modules:
  0.0 54.9 jit_solution(5148027307531900638)
XLA Ops:
  0.6 53.6 %shard_map.122 = (f32[12,8,192]{2,1,0:T(8,128)S(1)}, f32[12,8,192]{2,1,0:T(8,128)S(1)}) custom-call(f32[12,8,192]{2,1,0:T(8,128)} %coarse_hbm.1, f32[4,8,192]{2,1,0:T(8,128)} %static_hbm.1, s32[64]{0:T(128)} %seeds.1, bf16[9,16,128]{2,1,0:T(8,128)(2,1)} %bitcast.18, bf16[1152,128]{1,0:T(8,128)(2,1)} %bitcast.14, bf16[1152,128]{1,0:T(8,128)(2,1)} %bitcast.15, ...), custom_call_target="tpu_custom_call" | custom-call | tf_op jit(solution)/shard_map/pallas_call | solution.py:771
  54.2 0.7 %shard_map.123 = (f32[12,8,192]{2,1,0:T(8,128)}, f32[12,8,192]{2,1,0:T(8,128)}) custom-call(f32[12,8,192]{2,1,0:T(8,128)S(1)} %get-tuple-element.4.mean_in, f32[12,8,192]{2,1,0:T(8,128)S(1)} %get-tuple-element.5.field_in), custom_call_target="tpu_custom_call" | custom-call | tf_op jit(solution)/shard_map/pallas_call | solution.py:843
